TPU v7x, 32 devices: a whole 2x2x4 slice. The times are simulated.
32 devices in a mesh: section: 4 (over x, core), ctx: 8 (over z, y).
Axes of the slice: x: 2, y: 2, z: 4, core: 2. Of those that a mesh axis runs over, the one named last changes fastest.
Arguments:
- queries: bfloat16 [4, 1024, 2048], P('section', 'ctx'), may hold values from -6 to 6
- keys: bfloat16 [4, 1024, 512], P('section', 'ctx'), may hold values from -6 to 6
- values: bfloat16 [4, 1024, 512], P('section', 'ctx'), may hold values from -6 to 6
- outputs: bfloat16 [4, 1024, 2048], P('section', 'ctx'), may hold values from -2 to 2
- upstream: bfloat16 [4, 1024, 2048], P('section', 'ctx'), may hold values from -6 to 6
- lse: float32 [4, 16, 1024], P('section', None, 'ctx'), may hold values from 3 to 6
- span_ids: int32 [16], P('ctx'), may hold values from 0 to 15, as said below
Outputs:
- grad_queries: bfloat16 [4, 1024, 2048], P('section', 'ctx')
- window_key_gradient: bfloat16 [4, 1024, 512], P('section', 'ctx')
- window_value_gradient: bfloat16 [4, 1024, 512], P('section', 'ctx')
Inputs may be any that keep to these rules, and one draw needn't show every extreme that they name: `span_ids`: for each shard n, entries 2 n and 2 n + 1 are c and 15 - c for some c < 8; every span appears once.
All inputs are finite; a program needn't handle non-finite values.
Results may differ from a plain program's by a relative error of at most 0.0051.
Values may be sent and summed in bfloat16 or wider, within the bound.
A program may use at most 64 MiB of HBM per device.

v0:
```python
import jax
import jax.numpy as jnp
from jax import lax
from jax.sharding import PartitionSpec as P

QUERY_HEADS = 16
KEY_VALUE_HEADS = 4
HEAD_WIDTH = 128
CYCLE = 4


def from_behind(value, axis, steps):
    count = lax.axis_size(axis)
    pairs = [(source, (source + steps) % count) for source in range(count)]
    return lax.ppermute(value, axis, pairs)


def shard_positions(table, source, query_rows):
    half = query_rows // 2
    pair = lax.dynamic_slice(table, (2 * source,), (2,))
    local = jnp.arange(query_rows)
    chosen = jnp.where(local < half, pair[0], pair[1])
    return chosen * half + local % half


def block_terms(
    head_queries, head_gradient, delta, row_logsumexp, my_pos, key_now, value_now, key_pos
):
    scale = HEAD_WIDTH ** (-0.5)
    score = (
        jnp.einsum("qhgd,khd->hgqk", head_queries, key_now, preferred_element_type=jnp.float32)
        * scale
    )
    allowed = key_pos[None, None, None, :] <= my_pos[None, None, :, None]
    prob = jnp.where(allowed, jnp.exp(score - row_logsumexp[..., None]), jnp.float32(0.0))
    prob_b = prob.astype(jnp.bfloat16)
    dvalue = jnp.einsum("hgqk,qhgd->khd", prob_b, head_gradient, preferred_element_type=jnp.float32)
    dprob = jnp.einsum(
        "qhgd,khd->hgqk", head_gradient, value_now, preferred_element_type=jnp.float32
    )
    dscore_b = (prob * (dprob - delta[..., None]) * scale).astype(jnp.bfloat16)
    dquery = jnp.einsum("hgqk,khd->qhgd", dscore_b, key_now, preferred_element_type=jnp.float32)
    dkey = jnp.einsum("hgqk,qhgd->khd", dscore_b, head_queries, preferred_element_type=jnp.float32)
    return (dquery, dkey, dvalue)


def body(queries, keys, values, outputs, upstream, lse, span_ids):
    query_group = QUERY_HEADS // KEY_VALUE_HEADS
    query_rows = queries.shape[1]
    output_gradient = from_behind(upstream, "section", -1)
    table = lax.all_gather(span_ids, "ctx", axis=0, tiled=True)
    count = lax.axis_size("ctx")
    myself = lax.axis_index("ctx")
    head_queries = queries[0].reshape(query_rows, KEY_VALUE_HEADS, query_group, HEAD_WIDTH)
    head_gradient = output_gradient[0].reshape(query_rows, KEY_VALUE_HEADS, query_group, HEAD_WIDTH)
    head_output = outputs[0].reshape(query_rows, KEY_VALUE_HEADS, query_group, HEAD_WIDTH)
    delta = jnp.einsum(
        "qhgd,qhgd->hgq", head_gradient, head_output, preferred_element_type=jnp.float32
    )
    row_logsumexp = lse[0].reshape(KEY_VALUE_HEADS, query_group, query_rows)
    my_pos = shard_positions(table, myself, query_rows)
    visiting_block = (
        keys[0].reshape(query_rows, KEY_VALUE_HEADS, HEAD_WIDTH),
        values[0].reshape(query_rows, KEY_VALUE_HEADS, HEAD_WIDTH),
    )
    query_gradient = jnp.zeros((query_rows, KEY_VALUE_HEADS, query_group, HEAD_WIDTH), jnp.float32)
    carried_state = (
        jnp.zeros((query_rows, KEY_VALUE_HEADS, HEAD_WIDTH), jnp.float32),
        jnp.zeros((query_rows, KEY_VALUE_HEADS, HEAD_WIDTH), jnp.float32),
    )
    for step in range(CYCLE + 1):
        if step > 0:
            visiting_block = from_behind((visiting_block[0], visiting_block[1]), "ctx", 1)
            carried_state = from_behind((carried_state[0], carried_state[1]), "ctx", 1)
        source = (myself - step) % count
        key_pos = shard_positions(table, source, query_rows)
        dquery, dkey, dvalue = block_terms(
            head_queries,
            head_gradient,
            delta,
            row_logsumexp,
            my_pos,
            visiting_block[0],
            visiting_block[1],
            key_pos,
        )
        query_gradient = query_gradient + dquery
        carried_state = (carried_state[0] + dkey, carried_state[1] + dvalue)
    carried_state = (
        from_behind(carried_state[0].astype(jnp.bfloat16), "ctx", -CYCLE).astype(jnp.float32),
        from_behind(carried_state[1].astype(jnp.bfloat16), "ctx", -CYCLE).astype(jnp.float32),
    )
    grad_queries = query_gradient.reshape(1, query_rows, QUERY_HEADS * HEAD_WIDTH).astype(
        jnp.bfloat16
    )
    window_key_gradient = (
        carried_state[0].reshape(1, query_rows, KEY_VALUE_HEADS * HEAD_WIDTH).astype(jnp.bfloat16)
    )
    window_value_gradient = (
        carried_state[1].reshape(1, query_rows, KEY_VALUE_HEADS * HEAD_WIDTH).astype(jnp.bfloat16)
    )
    return (grad_queries, window_key_gradient, window_value_gradient)


def solution(mesh):
    placed = (
        P("section", "ctx", None),
        P("section", "ctx", None),
        P("section", "ctx", None),
        P("section", "ctx", None),
        P("section", "ctx", None),
        P("section", None, "ctx"),
        P("ctx"),
    )
    return jax.shard_map(
        body,
        mesh=mesh,
        in_specs=placed,
        out_specs=(P("section", "ctx", None), P("section", "ctx", None), P("section", "ctx", None)),
        check_vma=False,
    )
```

profile of v0, /device:TPU:0, one launch (start us, length us, event | category | flops | bytes accessed | tf_op | source)
XLA Modules:
  0.0 118.4 jit_solution(15756076497743763354)
XLA Ops:
  1.9 3.0 %collective-permute-start.1 = (bf16[128,4,128]{2,0,1:T(8,128)(2,1)S(1)}, bf16[128,4,128]{2,0,1:T(8,128)(2,1)S(1)}, u32[]{:S(2)}, u32[]{:S(2)}) collective-permute-start(bf16[128,4,128]{2,0,1:T(8,128)(2,1)S(1)} %copy.39), channel_id=1, source_target_pairs={{0,1},{1,2},{2,3},{3,4},{4,5},{5,6},{6,7},{7,0},{8,9},{9,10},{10,1... | collective-permute-start | bytes 393224 | tf_op jit(solution)/shard_map/ppermute | solution.py:15
  6.1 1.6 %collective-permute-start.2 = (bf16[128,4,128]{2,0,1:T(8,128)(2,1)S(1)}, bf16[128,4,128]{2,0,1:T(8,128)(2,1)S(1)}, u32[]{:S(2)}, u32[]{:S(2)}) collective-permute-start(bf16[128,4,128]{2,0,1:T(8,128)(2,1)S(1)} %copy.41), channel_id=1, source_target_pairs={{0,1},{1,2},{2,3},{3,4},{4,5},{5,6},{6,7},{7,0},{8,9},{9,10},{10,1... | collective-permute-start | bytes 393224 | tf_op jit(solution)/shard_map/ppermute | solution.py:15
  11.1 10.4 %all-reduce = s32[16]{0:T(128)S(1)} all-reduce(s32[16]{0:T(128)S(1)} %dynamic-update-slice), channel_id=1, replica_groups=mesh['section'=4,'ctx'=8] {'ctx'}, use_global_device_ids=true, to_apply=%add | all-reduce | flops 16 | bytes 128
  32.2 1.4 %fusion.34 = f32[4,4,128,128]{2,3,1,0:T(8,128)} fusion(bf16[128,4,128,1]{0,2,3,1:T(8,128)(2,1)S(1)} %bitcast.277, f32[4,4,128]{2,1,0:T(4,128)S(1)} %bitcast.281, pred[128,128]{0,1:T(8,128)(4,1)S(1)} %get-tuple-element.13, bf16[128,4,4,128]{3,2,1,0:T(4,128)(2,1)S(1)} %reshape_squeeze.16), kind=kOutput, calls=%fused_computation.48 | convolution fusion | flops 67895296 | bytes 1728512 | tf_op jit(solution)/shard_map/qhgd,khd->hgqk/dot_general | solution.py:31
  34.7 1.4 %collective-permute-start.3 = (bf16[128,4,128]{2,0,1:T(8,128)(2,1)S(1)}, bf16[128,4,128]{2,0,1:T(8,128)(2,1)S(1)}, u32[]{:S(2)}, u32[]{:S(2)}) collective-permute-start(bf16[128,4,128]{2,0,1:T(8,128)(2,1)S(1)} %collective-permute-done.1), channel_id=1, source_target_pairs={{0,1},{1,2},{2,3},{3,4},{4,5},{5,6},{6,7},{7,0},{8,9},{9,10},{10,1... | collective-permute-start | bytes 393224 | tf_op jit(solution)/shard_map/ppermute | solution.py:15
  36.1 1.7 %collective-permute-start.4 = (bf16[128,4,128]{2,0,1:T(8,128)(2,1)S(1)}, bf16[128,4,128]{2,0,1:T(8,128)(2,1)S(1)}, u32[]{:S(2)}, u32[]{:S(2)}) collective-permute-start(bf16[128,4,128]{2,0,1:T(8,128)(2,1)S(1)} %collective-permute-done.2), channel_id=1, source_target_pairs={{0,1},{1,2},{2,3},{3,4},{4,5},{5,6},{6,7},{7,0},{8,9},{9,10},{10,1... | collective-permute-start | bytes 393224 | tf_op jit(solution)/shard_map/ppermute | solution.py:15
  37.9 1.3 %fusion.27 = f32[4,4,128,128]{2,3,1,0:T(8,128)} fusion(f32[4,4,128]{2,1,0:T(4,128)S(1)} %bitcast.282, pred[128,128]{0,1:T(8,128)(4,1)S(1)} %get-tuple-element.10, bf16[128,4,128]{2,0,1:T(8,128)(2,1)S(1)} %collective-permute-done.1, bf16[128,4,4,128]{3,2,1,0:T(4,128)(2,1)S(1)} %reshape_squeeze.16), kind=kOutput, calls=%fused_computation.39 | convolution fusion | flops 67895296 | bytes 1728512 | tf_op jit(solution)/shard_map/qhgd,khd->hgqk/dot_general | solution.py:31
  39.2 3.2 %collective-permute-done.3 = bf16[128,4,128]{2,0,1:T(8,128)(2,1)S(1)} collective-permute-done((bf16[128,4,128]{2,0,1:T(8,128)(2,1)S(1)}, bf16[128,4,128]{2,0,1:T(8,128)(2,1)S(1)}, u32[]{:S(2)}, u32[]{:S(2)}) %collective-permute-start.3) | collective-permute-done | bytes 131104 | tf_op jit(solution)/shard_map/ppermute | solution.py:15
  42.4 1.4 %collective-permute-done.4 = bf16[128,4,128]{2,0,1:T(8,128)(2,1)S(1)} collective-permute-done((bf16[128,4,128]{2,0,1:T(8,128)(2,1)S(1)}, bf16[128,4,128]{2,0,1:T(8,128)(2,1)S(1)}, u32[]{:S(2)}, u32[]{:S(2)}) %collective-permute-start.4) | collective-permute-done | bytes 131104 | tf_op jit(solution)/shard_map/ppermute | solution.py:15
  44.2 1.4 %fusion.20 = f32[4,4,128,128]{2,3,1,0:T(8,128)} fusion(f32[4,4,128]{2,1,0:T(4,128)S(1)} %bitcast.283, pred[128,128]{0,1:T(8,128)(4,1)S(1)} %get-tuple-element.11, bf16[128,4,128]{2,0,1:T(8,128)(2,1)S(1)} %collective-permute-done.3, bf16[128,4,4,128]{3,2,1,0:T(4,128)(2,1)S(1)} %reshape_squeeze.16), kind=kOutput, calls=%fused_computation.29 | convolution fusion | flops 67895296 | bytes 1728512 | tf_op jit(solution)/shard_map/qhgd,khd->hgqk/dot_general | solution.py:31
  45.6 4.6 %collective-permute-done.5 = bf16[128,4,128]{2,0,1:T(8,128)(2,1)} collective-permute-done((bf16[128,4,128]{2,0,1:T(8,128)(2,1)S(1)}, bf16[128,4,128]{2,0,1:T(8,128)(2,1)}, u32[]{:S(2)}, u32[]{:S(2)}) %collective-permute-start.5) | collective-permute-done | bytes 131104 | tf_op jit(solution)/shard_map/ppermute | solution.py:15
  50.2 2.2 %collective-permute-done.6 = bf16[128,4,128]{2,0,1:T(8,128)(2,1)} collective-permute-done((bf16[128,4,128]{2,0,1:T(8,128)(2,1)S(1)}, bf16[128,4,128]{2,0,1:T(8,128)(2,1)}, u32[]{:S(2)}, u32[]{:S(2)}) %collective-permute-start.6) | collective-permute-done | bytes 131104 | tf_op jit(solution)/shard_map/ppermute | solution.py:15
  54.2 2.4 %multiply_reduce_fusion = f32[4,4,128]{1,0,2:T(4,128)} fusion(f32[4,4,128,128]{3,1,0,2:T(4,128)S(1)} %copy.80, bf16[128,4,4,128]{3,2,1,0:T(4,128)(2,1)} %reshape_squeeze.19), kind=kLoop, calls=%fused_computation.66 | loop fusion | flops 784384 | bytes 1581056
  57.7 1.5 %convolution_bitcast_fusion.9 = f32[128,4,128]{2,0,1:T(8,128)S(1)} fusion(bf16[128,4,4,128]{0,3,2,1:T(8,128)(2,1)S(1)} %bitcast.263, f32[4,4,128,128]{2,3,1,0:T(8,128)} %fusion.34), kind=kOutput, calls=%fused_computation.59 | convolution fusion | flops 67371008 | bytes 1835008 | tf_op jit(solution)/shard_map/hgqk,qhgd->khd/dot_general | solution.py:37
  60.3 1.9 %collective-permute-start.14 = (f32[128,4,128]{2,0,1:T(8,128)S(1)}, f32[128,4,128]{2,0,1:T(8,128)S(1)}, u32[]{:S(2)}, u32[]{:S(2)}) collective-permute-start(f32[128,4,128]{2,0,1:T(8,128)S(1)} %convolution_bitcast_fusion.9), channel_id=1, source_target_pairs={{0,1},{1,2},{2,3},{3,4},{4,5},{5,6},{6,7},{7,0},{8,9},{9,10},{10,1... | collective-permute-start | bytes 786440 | tf_op jit(solution)/shard_map/ppermute | solution.py:15
  72.1 3.3 %collective-permute-done.9 = f32[128,4,128]{2,0,1:T(8,128)S(1)} collective-permute-done((f32[128,4,128]{2,0,1:T(8,128)S(1)}, f32[128,4,128]{2,0,1:T(8,128)S(1)}, u32[]{:S(2)}, u32[]{:S(2)}) %collective-permute-start.9) | collective-permute-done | bytes 262176 | tf_op jit(solution)/shard_map/ppermute | solution.py:15
  76.0 5.0 %collective-permute-done.15 = f32[128,4,128]{2,0,1:T(8,128)S(1)} collective-permute-done((f32[128,4,128]{2,0,1:T(8,128)S(1)}, f32[128,4,128]{2,0,1:T(8,128)S(1)}, u32[]{:S(2)}, u32[]{:S(2)}) %collective-permute-start.15) | collective-permute-done | bytes 262176 | tf_op jit(solution)/shard_map/ppermute | solution.py:15
  81.7 5.9 %collective-permute-done.10 = f32[128,4,128]{2,0,1:T(8,128)S(1)} collective-permute-done((f32[128,4,128]{2,0,1:T(8,128)S(1)}, f32[128,4,128]{2,0,1:T(8,128)S(1)}, u32[]{:S(2)}, u32[]{:S(2)}) %collective-permute-start.10) | collective-permute-done | bytes 262176 | tf_op jit(solution)/shard_map/ppermute | solution.py:15
  88.0 5.2 %collective-permute-done.16 = f32[128,4,128]{2,0,1:T(8,128)S(1)} collective-permute-done((f32[128,4,128]{2,0,1:T(8,128)S(1)}, f32[128,4,128]{2,0,1:T(8,128)S(1)}, u32[]{:S(2)}, u32[]{:S(2)}) %collective-permute-start.16) | collective-permute-done | bytes 262176 | tf_op jit(solution)/shard_map/ppermute | solution.py:15
  93.7 5.4 %collective-permute-done.11 = f32[128,4,128]{2,0,1:T(8,128)S(1)} collective-permute-done((f32[128,4,128]{2,0,1:T(8,128)S(1)}, f32[128,4,128]{2,0,1:T(8,128)S(1)}, u32[]{:S(2)}, u32[]{:S(2)}) %collective-permute-start.11) | collective-permute-done | bytes 262176 | tf_op jit(solution)/shard_map/ppermute | solution.py:15
  99.4 5.2 %collective-permute-done.17 = f32[128,4,128]{2,0,1:T(8,128)S(1)} collective-permute-done((f32[128,4,128]{2,0,1:T(8,128)S(1)}, f32[128,4,128]{2,0,1:T(8,128)S(1)}, u32[]{:S(2)}, u32[]{:S(2)}) %collective-permute-start.17) | collective-permute-done | bytes 262176 | tf_op jit(solution)/shard_map/ppermute | solution.py:15
  104.7 2.5 %collective-permute-start.18 = (bf16[128,4,128]{2,0,1:T(8,128)(2,1)S(1)}, bf16[128,4,128]{2,0,1:T(8,128)(2,1)S(1)}, u32[]{:S(2)}, u32[]{:S(2)}) collective-permute-start(bf16[128,4,128]{2,0,1:T(8,128)(2,1)S(1)} %add_convert_fusion), channel_id=1, source_target_pairs={{0,4},{1,5},{2,6},{3,7},{4,0},{5,1},{6,2},{7,3},{8,12},{9,13},{10,... | collective-permute-start | bytes 393224 | tf_op jit(solution)/shard_map/ppermute | solution.py:15
  107.2 1.8 %collective-permute-done.12 = f32[128,4,128]{2,0,1:T(8,128)S(1)} collective-permute-done((f32[128,4,128]{2,0,1:T(8,128)S(1)}, f32[128,4,128]{2,0,1:T(8,128)S(1)}, u32[]{:S(2)}, u32[]{:S(2)}) %collective-permute-start.12) | collective-permute-done | bytes 262176 | tf_op jit(solution)/shard_map/ppermute | solution.py:15
  109.0 5.3 %collective-permute-start.13 = (bf16[128,4,128]{2,0,1:T(8,128)(2,1)S(1)}, bf16[128,4,128]{2,0,1:T(8,128)(2,1)S(1)}, u32[]{:S(2)}, u32[]{:S(2)}) collective-permute-start(bf16[128,4,128]{2,0,1:T(8,128)(2,1)S(1)} %add_convert_fusion.1), channel_id=1, source_target_pairs={{0,4},{1,5},{2,6},{3,7},{4,0},{5,1},{6,2},{7,3},{8,12},{9,13},{10,... | collective-permute-start | bytes 393224 | tf_op jit(solution)/shard_map/ppermute | solution.py:15
  (108 shorter events, 37.6 us)
Async XLA Ops:
  0.6 7.0 %copy-start.3 = (bf16[1,128,2048]{2,1,0:T(8,128)(2,1)S(1)}, bf16[1,128,2048]{2,1,0:T(8,128)(2,1)}, u32[]{:S(2)}) copy-start(bf16[1,128,2048]{2,1,0:T(8,128)(2,1)} %param.11) | copy-start | bytes 1572868
  1.9 32.9 %collective-permute-start.1 = (bf16[128,4,128]{2,0,1:T(8,128)(2,1)S(1)}, bf16[128,4,128]{2,0,1:T(8,128)(2,1)S(1)}, u32[]{:S(2)}, u32[]{:S(2)}) collective-permute-start(bf16[128,4,128]{2,0,1:T(8,128)(2,1)S(1)} %copy.39), channel_id=1, source_target_pairs={{0,1},{1,2},{2,3},{3,4},{4,5},{5,6},{6,7},{7,0},{8,9},{9,10},{10,1... | collective-permute-start | bytes 393224 | tf_op jit(solution)/shard_map/ppermute | solution.py:15
  6.1 15.4 %copy-start.4 = (bf16[1,128,2048]{2,1,0:T(8,128)(2,1)S(1)}, bf16[1,128,2048]{2,1,0:T(8,128)(2,1)}, u32[]{:S(2)}) copy-start(bf16[1,128,2048]{2,1,0:T(8,128)(2,1)} %param.7) | copy-start | bytes 1572868
  6.1 30.1 %collective-permute-start.2 = (bf16[128,4,128]{2,0,1:T(8,128)(2,1)S(1)}, bf16[128,4,128]{2,0,1:T(8,128)(2,1)S(1)}, u32[]{:S(2)}, u32[]{:S(2)}) collective-permute-start(bf16[128,4,128]{2,0,1:T(8,128)(2,1)S(1)} %copy.41), channel_id=1, source_target_pairs={{0,1},{1,2},{2,3},{3,4},{4,5},{5,6},{6,7},{7,0},{8,9},{9,10},{10,1... | collective-permute-start | bytes 393224 | tf_op jit(solution)/shard_map/ppermute | solution.py:15
  7.9 45.7 %collective-permute-start = (bf16[1,128,2048]{1,2,0:T(8,128)(2,1)S(1)}, bf16[1,128,2048]{1,2,0:T(8,128)(2,1)S(1)}, u32[]{:S(2)}, u32[]{:S(2)}) collective-permute-start(bf16[1,128,2048]{1,2,0:T(8,128)(2,1)S(1)} %copy.35), channel_id=1, source_target_pairs={{0,24},{8,0},{16,8},{24,16},{1,25},{9,1},{17,9},{25,17},{2,26},{10... | collective-permute-start | bytes 1572872 | tf_op jit(solution)/shard_map/ppermute | solution.py:15
  34.7 4.5 %copy-start.8 = (bf16[128,4,128]{2,0,1:T(8,128)(2,1)}, bf16[128,4,128]{2,0,1:T(8,128)(2,1)S(1)}, u32[]{:S(2)}) copy-start(bf16[128,4,128]{2,0,1:T(8,128)(2,1)S(1)} %collective-permute-done.1) | copy-start | bytes 393220
  34.7 7.7 %collective-permute-start.3 = (bf16[128,4,128]{2,0,1:T(8,128)(2,1)S(1)}, bf16[128,4,128]{2,0,1:T(8,128)(2,1)S(1)}, u32[]{:S(2)}, u32[]{:S(2)}) collective-permute-start(bf16[128,4,128]{2,0,1:T(8,128)(2,1)S(1)} %collective-permute-done.1), channel_id=1, source_target_pairs={{0,1},{1,2},{2,3},{3,4},{4,5},{5,6},{6,7},{7,0},{8,9},{9,10},{10,1... | collective-permute-start | bytes 393224 | tf_op jit(solution)/shard_map/ppermute | solution.py:15
  36.1 7.7 %collective-permute-start.4 = (bf16[128,4,128]{2,0,1:T(8,128)(2,1)S(1)}, bf16[128,4,128]{2,0,1:T(8,128)(2,1)S(1)}, u32[]{:S(2)}, u32[]{:S(2)}) collective-permute-start(bf16[128,4,128]{2,0,1:T(8,128)(2,1)S(1)} %collective-permute-done.2), channel_id=1, source_target_pairs={{0,1},{1,2},{2,3},{3,4},{4,5},{5,6},{6,7},{7,0},{8,9},{9,10},{10,1... | collective-permute-start | bytes 393224 | tf_op jit(solution)/shard_map/ppermute | solution.py:15
  42.4 3.2 %copy-start.10 = (bf16[128,4,128]{2,0,1:T(8,128)(2,1)}, bf16[128,4,128]{2,0,1:T(8,128)(2,1)S(1)}, u32[]{:S(2)}) copy-start(bf16[128,4,128]{2,0,1:T(8,128)(2,1)S(1)} %collective-permute-done.3) | copy-start | bytes 393220
  42.4 7.8 %collective-permute-start.5 = (bf16[128,4,128]{2,0,1:T(8,128)(2,1)S(1)}, bf16[128,4,128]{2,0,1:T(8,128)(2,1)}, u32[]{:S(2)}, u32[]{:S(2)}) collective-permute-start(bf16[128,4,128]{2,0,1:T(8,128)(2,1)S(1)} %collective-permute-done.3), channel_id=1, source_target_pairs={{0,1},{1,2},{2,3},{3,4},{4,5},{5,6},{6,7},{7,0},{8,9},{9,10},{10,1... | collective-permute-start | bytes 393224 | tf_op jit(solution)/shard_map/ppermute | solution.py:15
  43.8 8.5 %collective-permute-start.6 = (bf16[128,4,128]{2,0,1:T(8,128)(2,1)S(1)}, bf16[128,4,128]{2,0,1:T(8,128)(2,1)}, u32[]{:S(2)}, u32[]{:S(2)}) collective-permute-start(bf16[128,4,128]{2,0,1:T(8,128)(2,1)S(1)} %collective-permute-done.4), channel_id=1, source_target_pairs={{0,1},{1,2},{2,3},{3,4},{4,5},{5,6},{6,7},{7,0},{8,9},{9,10},{10,1... | collective-permute-start | bytes 393224 | tf_op jit(solution)/shard_map/ppermute | solution.py:15
  50.2 14.9 %collective-permute-start.7 = (bf16[128,4,128]{2,0,1:T(8,128)(2,1)}, bf16[128,4,128]{2,0,1:T(8,128)(2,1)}, u32[]{:S(2)}, u32[]{:S(2)}) collective-permute-start(bf16[128,4,128]{2,0,1:T(8,128)(2,1)} %collective-permute-done.5), channel_id=1, source_target_pairs={{0,1},{1,2},{2,3},{3,4},{4,5},{5,6},{6,7},{7,0},{8,9},{9,10},{10,1... | collective-permute-start | bytes 393224 | tf_op jit(solution)/shard_map/ppermute | solution.py:15
  52.3 17.3 %collective-permute-start.8 = (bf16[128,4,128]{2,0,1:T(8,128)(2,1)}, bf16[128,4,128]{2,0,1:T(8,128)(2,1)}, u32[]{:S(2)}, u32[]{:S(2)}) collective-permute-start(bf16[128,4,128]{2,0,1:T(8,128)(2,1)} %collective-permute-done.6), channel_id=1, source_target_pairs={{0,1},{1,2},{2,3},{3,4},{4,5},{5,6},{6,7},{7,0},{8,9},{9,10},{10,1... | collective-permute-start | bytes 393224 | tf_op jit(solution)/shard_map/ppermute | solution.py:15
  60.3 3.0 %copy-start = (f32[4,4,128,128]{2,3,1,0:T(8,128)S(1)}, f32[4,4,128,128]{2,3,1,0:T(8,128)}, u32[]{:S(2)}) copy-start(f32[4,4,128,128]{2,3,1,0:T(8,128)} %fusion.20) | copy-start | bytes 3145732
  60.3 10.6 %collective-permute-start.14 = (f32[128,4,128]{2,0,1:T(8,128)S(1)}, f32[128,4,128]{2,0,1:T(8,128)S(1)}, u32[]{:S(2)}, u32[]{:S(2)}) collective-permute-start(f32[128,4,128]{2,0,1:T(8,128)S(1)} %convolution_bitcast_fusion.9), channel_id=1, source_target_pairs={{0,1},{1,2},{2,3},{3,4},{4,5},{5,6},{6,7},{7,0},{8,9},{9,10},{10,1... | collective-permute-start | bytes 786440 | tf_op jit(solution)/shard_map/ppermute | solution.py:15
  62.2 13.2 %collective-permute-start.9 = (f32[128,4,128]{2,0,1:T(8,128)S(1)}, f32[128,4,128]{2,0,1:T(8,128)S(1)}, u32[]{:S(2)}, u32[]{:S(2)}) collective-permute-start(f32[128,4,128]{2,0,1:T(8,128)S(1)} %convolution_bitcast_fusion.14), channel_id=1, source_target_pairs={{0,1},{1,2},{2,3},{3,4},{4,5},{5,6},{6,7},{7,0},{8,9},{9,10},{10,1... | collective-permute-start | bytes 786440 | tf_op jit(solution)/shard_map/ppermute | solution.py:15
  70.9 10.1 %collective-permute-start.15 = (f32[128,4,128]{2,0,1:T(8,128)S(1)}, f32[128,4,128]{2,0,1:T(8,128)S(1)}, u32[]{:S(2)}, u32[]{:S(2)}) collective-permute-start(f32[128,4,128]{2,0,1:T(8,128)S(1)} %add.195), channel_id=1, source_target_pairs={{0,1},{1,2},{2,3},{3,4},{4,5},{5,6},{6,7},{7,0},{8,9},{9,10},{10,1... | collective-permute-start | bytes 786440 | tf_op jit(solution)/shard_map/ppermute | solution.py:15
  75.6 12.0 %collective-permute-start.10 = (f32[128,4,128]{2,0,1:T(8,128)S(1)}, f32[128,4,128]{2,0,1:T(8,128)S(1)}, u32[]{:S(2)}, u32[]{:S(2)}) collective-permute-start(f32[128,4,128]{2,0,1:T(8,128)S(1)} %fusion.41), channel_id=1, source_target_pairs={{0,1},{1,2},{2,3},{3,4},{4,5},{5,6},{6,7},{7,0},{8,9},{9,10},{10,1... | collective-permute-start | bytes 786440 | tf_op jit(solution)/shard_map/ppermute | solution.py:15
  81.1 12.2 %collective-permute-start.16 = (f32[128,4,128]{2,0,1:T(8,128)S(1)}, f32[128,4,128]{2,0,1:T(8,128)S(1)}, u32[]{:S(2)}, u32[]{:S(2)}) collective-permute-start(f32[128,4,128]{2,0,1:T(8,128)S(1)} %add.196), channel_id=1, source_target_pairs={{0,1},{1,2},{2,3},{3,4},{4,5},{5,6},{6,7},{7,0},{8,9},{9,10},{10,1... | collective-permute-start | bytes 786440 | tf_op jit(solution)/shard_map/ppermute | solution.py:15
  87.7 11.3 %collective-permute-start.11 = (f32[128,4,128]{2,0,1:T(8,128)S(1)}, f32[128,4,128]{2,0,1:T(8,128)S(1)}, u32[]{:S(2)}, u32[]{:S(2)}) collective-permute-start(f32[128,4,128]{2,0,1:T(8,128)S(1)} %add.192), channel_id=1, source_target_pairs={{0,1},{1,2},{2,3},{3,4},{4,5},{5,6},{6,7},{7,0},{8,9},{9,10},{10,1... | collective-permute-start | bytes 786440 | tf_op jit(solution)/shard_map/ppermute | solution.py:15
  93.3 11.3 %collective-permute-start.17 = (f32[128,4,128]{2,0,1:T(8,128)S(1)}, f32[128,4,128]{2,0,1:T(8,128)S(1)}, u32[]{:S(2)}, u32[]{:S(2)}) collective-permute-start(f32[128,4,128]{2,0,1:T(8,128)S(1)} %add.197), channel_id=1, source_target_pairs={{0,1},{1,2},{2,3},{3,4},{4,5},{5,6},{6,7},{7,0},{8,9},{9,10},{10,1... | collective-permute-start | bytes 786440 | tf_op jit(solution)/shard_map/ppermute | solution.py:15
  99.0 9.9 %collective-permute-start.12 = (f32[128,4,128]{2,0,1:T(8,128)S(1)}, f32[128,4,128]{2,0,1:T(8,128)S(1)}, u32[]{:S(2)}, u32[]{:S(2)}) collective-permute-start(f32[128,4,128]{2,0,1:T(8,128)S(1)} %add.193), channel_id=1, source_target_pairs={{0,1},{1,2},{2,3},{3,4},{4,5},{5,6},{6,7},{7,0},{8,9},{9,10},{10,1... | collective-permute-start | bytes 786440 | tf_op jit(solution)/shard_map/ppermute | solution.py:15
  104.7 11.9 %collective-permute-start.18 = (bf16[128,4,128]{2,0,1:T(8,128)(2,1)S(1)}, bf16[128,4,128]{2,0,1:T(8,128)(2,1)S(1)}, u32[]{:S(2)}, u32[]{:S(2)}) collective-permute-start(bf16[128,4,128]{2,0,1:T(8,128)(2,1)S(1)} %add_convert_fusion), channel_id=1, source_target_pairs={{0,4},{1,5},{2,6},{3,7},{4,0},{5,1},{6,2},{7,3},{8,12},{9,13},{10,... | collective-permute-start | bytes 393224 | tf_op jit(solution)/shard_map/ppermute | solution.py:15
  109.0 8.5 %collective-permute-start.13 = (bf16[128,4,128]{2,0,1:T(8,128)(2,1)S(1)}, bf16[128,4,128]{2,0,1:T(8,128)(2,1)S(1)}, u32[]{:S(2)}, u32[]{:S(2)}) collective-permute-start(bf16[128,4,128]{2,0,1:T(8,128)(2,1)S(1)} %add_convert_fusion.1), channel_id=1, source_target_pairs={{0,4},{1,5},{2,6},{3,7},{4,0},{5,1},{6,2},{7,3},{8,12},{9,13},{10,... | collective-permute-start | bytes 393224 | tf_op jit(solution)/shard_map/ppermute | solution.py:15
  (11 other events, 16.9 us)
where the time goes:
time: 119 us; the launch traced here: 118 us
  waiting for transfers between devices  43.1 us (36%)
  starting transfers between devices  20.8 us (17%)
  matrix products  17.6 us (15%)
  local copies, waits for them, and re-layouts  13.6 us (11%)
  other arithmetic  11 us (9%)
  blocking collectives  10.4 us (9%)
  between operations  1.79 us (2%)
    ppermute x19, waiting for transfers between devices, from_behind(): return lax.ppermute(value, axis, pairs)  43.1 us
    ppermute x19, starting transfers between devices, from_behind(): return lax.ppermute(value, axis, pairs)  20.8 us
    unnamed x1, blocking collectives  10.4 us
    unnamed x42, local copies, waits for them, and re-layouts  8.53 us
    add x6, other arithmetic, shard_positions(): return chosen * half + local % half  7.66 us
    dot_general x5, matrix products, block_terms(): jnp.einsum('qhgd,khd->hgqk', head_queries, key_now, preferred_element_typ...  6.65 us
    dot_general x5, matrix products, block_terms(): jnp.einsum('hgqk,khd->qhgd', dscore_b, key_now, preferred_element_type=jn...  3.46 us
    dot_general x5, matrix products, block_terms(): jnp.einsum('qhgd,khd->hgqk', head_gradient, value_now, preferred_element_...  3.33 us
  transfers between devices with their start and end apart: 19, of which 11 were waited for; matrix products, arithmetic and copies ran while one was open for 32% of the time, Pallas kernels for 0%

commit v1 on v0

v1 whole, which is shorter than its diff:
```python
import functools
import math

import jax
import jax.numpy as jnp
from jax import lax
from jax.experimental import pallas as pl
from jax.experimental.pallas import tpu as pltpu
from jax.sharding import PartitionSpec as P

G = 4
R = 4
D = 128
HEAD = 16
MESH = pl.DeviceIdType.MESH
F32 = jnp.float32
BF16 = jnp.bfloat16
C1, C2, X1, X3 = 0, 1, 2, 3


def dot(a, b, ca, cb):
    return lax.dot_general(a, b, (((ca,), (cb,)), ((), ())), preferred_element_type=F32)


def kernel(
    sections, count, span_ref, q_ref, k_ref, v_ref, o_ref, lse_ref, up_ref,
    dq_ref, dk_ref, dv_ref,
    kv, do, dqt, delta, pacc, gsend, grecv,
    up_s, up_r, kv_s, kv_r, g_s, g_r,
):
    T = q_ref.shape[1]
    half = T // 2
    sec = lax.axis_index("section")
    me = lax.axis_index("ctx")
    side = lax.rem(me, 2)
    sec_prev = lax.rem(sec + sections - 1, sections)
    sec_next = lax.rem(sec + 1, sections)
    above = lax.rem(me + 2, count)
    below = lax.rem(me + count - 2, count)
    partner = me + 1 - 2 * side

    s0 = span_ref[0]
    s1 = span_ref[1]

    rows = lax.broadcasted_iota(jnp.int32, (HEAD, D), 0)
    header = jnp.where(rows < HEAD // 2, s0, s1).astype(F32).astype(BF16)
    for g in range(G):
        kv[0, g, 0:HEAD, :] = header
        kv[0, g, HEAD : HEAD + T, :] = k_ref[0, :, g * D : (g + 1) * D]
        kv[0, g, HEAD + T : HEAD + 2 * T, :] = v_ref[0, :, g * D : (g + 1) * D]

    barrier = pltpu.get_barrier_semaphore()
    for axis, other in (
        ("ctx", above), ("ctx", below), ("ctx", partner),
        ("section", sec_prev), ("section", sec_next),
    ):
        pl.semaphore_signal(barrier, inc=1, device_id={axis: other}, device_id_type=MESH)
    pl.semaphore_wait(barrier, 5)

    def up_copy(g):
        return pltpu.make_async_remote_copy(
            src_ref=up_ref.at[0, :, pl.ds(pl.multiple_of(g * (R * D), R * D), R * D)],
            dst_ref=do.at[g], send_sem=up_s.at[g], recv_sem=up_r.at[g],
            device_id={"section": sec_prev}, device_id_type=MESH,
        )

    def kv_copy(t, src, g):
        return pltpu.make_async_remote_copy(
            src_ref=kv.at[src, g], dst_ref=kv.at[t + 1, g],
            send_sem=kv_s.at[t, g], recv_sem=kv_r.at[t, g],
            device_id={"ctx": above if t in (C1, C2) else partner}, device_id_type=MESH,
        )

    def g_copy(t, g):
        return pltpu.make_async_remote_copy(
            src_ref=gsend.at[t, g], dst_ref=grecv.at[t, g],
            send_sem=g_s.at[t, g], recv_sem=g_r.at[t, g],
            device_id={"ctx": below if t in (C1, C2) else partner}, device_id_type=MESH,
        )

    def loop(body):
        def step(g, carry):
            body(g)
            return carry

        lax.fori_loop(0, G, step, 0)

    def start_all(g):
        kv_copy(C1, 0, g).start()

        @pl.when(side == 0)
        def _():
            kv_copy(X1, 0, g).start()

        up_copy(g).start()

    loop(start_all)

    scale = D ** (-0.5)
    scale2 = scale * math.log2(math.e)
    krow = lax.broadcasted_iota(jnp.int32, (T, D), 0)
    kbase = jnp.where(krow < half, krow, krow - half).astype(F32)
    qlane = lax.broadcasted_iota(jnp.int32, (T, T), 1)
    qpos = (jnp.where(qlane < half, s0, s1) * half).astype(F32) + jnp.where(
        qlane < half, qlane, qlane - half
    ).astype(F32)

    def heads(ref, *at):
        return jnp.concatenate([ref[at + (slice(None), slice(j * D, (j + 1) * D))] for j in range(R)], axis=0)

    def q_heads(g):
        wide = q_ref[0, :, pl.ds(pl.multiple_of(g * (R * D), R * D), R * D)]
        return jnp.concatenate([wide[:, j * D : (j + 1) * D] for j in range(R)], axis=0)

    def block(g, slot, first=False):
        head = kv[slot, g, 0:HEAD, :].astype(F32)
        k = kv[slot, g, HEAD : HEAD + T, :]
        v = kv[slot, g, HEAD + T : HEAD + 2 * T, :]
        q4 = q_heads(g)
        do4 = heads(do, g)
        kpos = jnp.where(krow < half, head[0:1, :], head[8:9, :]) * half + kbase
        allowed = kpos <= qpos
        lse = jnp.concatenate(
            [lse_ref[0, pl.ds(g * R + j, 1), :] for j in range(R)], axis=1
        ) * math.log2(math.e)
        dl = delta[g, 0:1, :]
        s = dot(k, q4, 1, 1)
        e = jnp.exp2(s * scale2 - lse)
        p = jnp.where(jnp.concatenate([allowed] * R, axis=1), e, 0.0)
        dp = dot(v, do4, 1, 1)
        ds = (p * (dp - dl) * scale).astype(BF16)
        dval = dot(p.astype(BF16), do4, 1, 0)
        dkey = dot(ds, q4, 1, 0)
        term = dot(k, ds, 0, 0)
        if first:
            dqt[g] = term
        else:
            dqt[g] += term
        return dkey, dval

    def keep(g, slot, pair):
        pacc[slot, g, 0:T, :] = pair[0]
        pacc[slot, g, T : 2 * T, :] = pair[1]

    def pass_on(t, g, pair):
        gsend[t, g, 0:T, :] = pair[0].astype(BF16)
        gsend[t, g, T : 2 * T, :] = pair[1].astype(BF16)
        g_copy(t, g).start()

    def phase1(g):
        kv_copy(C1, 0, g).wait_recv()
        kv_copy(C2, 1, g).start()

        @pl.when(side == 0)
        def _():
            kv_copy(X3, 1, g).start()

        @pl.when(side == 1)
        def _():
            kv_copy(X1, 1, g).start()

        up_copy(g).wait_recv()
        o4 = o_ref[0, :, pl.ds(pl.multiple_of(g * (R * D), R * D), R * D)].astype(F32)
        prod = o4 * do[g].astype(F32)
        delta[g, 0:1, :] = jnp.concatenate(
            [jnp.sum(prod[:, j * D : (j + 1) * D].T, axis=0, keepdims=True) for j in range(R)], axis=1
        )
        keep(g, 0, block(g, 0, True))

    loop(phase1)

    def phase2(g):
        kv_copy(C2, 1, g).wait_recv()

        @pl.when(side == 1)
        def _():
            kv_copy(X3, 2, g).start()

        keep(g, 1, block(g, 1))

    loop(phase2)

    def phase3(g):
        kv_copy(X1, 0, g).wait_recv()
        pass_on(X1, g, block(g, 3))
        kv_copy(X3, 0, g).wait_recv()
        pass_on(X3, g, block(g, 4))
        keep(g, 2, block(g, 2))
        total = dqt[g]
        dq_ref[0, :, pl.ds(pl.multiple_of(g * (R * D), R * D), R * D)] = jnp.concatenate(
            [total[:, j * T : (j + 1) * T].T for j in range(R)], axis=1
        ).astype(BF16)

    loop(phase3)

    def phase4(g):
        g_copy(X1, g).wait_recv()
        pacc[side, g] += grecv[X1, g].astype(F32)
        g_copy(X3, g).wait_recv()
        pacc[side + 1, g] += grecv[X3, g].astype(F32)
        gsend[C2, g] = pacc[2, g].astype(BF16)
        g_copy(C2, g).start()

    loop(phase4)

    def phase5(g):
        g_copy(C2, g).wait_recv()
        gsend[C1, g] = (pacc[1, g] + grecv[C2, g].astype(F32)).astype(BF16)
        g_copy(C1, g).start()

    loop(phase5)

    def phase6(g):
        g_copy(C1, g).wait_recv()
        total = (pacc[0, g] + grecv[C1, g].astype(F32)).astype(BF16)
        at = pl.ds(pl.multiple_of(g * D, D), D)
        dk_ref[0, :, at] = total[0:T]
        dv_ref[0, :, at] = total[T : 2 * T]

    loop(phase6)

    def finish(g):
        up_copy(g).wait_send()
        for t in (C1, C2, X1, X3):
            kv_copy(t, 0, g).wait_send()
            g_copy(t, g).wait_send()

    loop(finish)


def body(mesh, queries, keys, values, outputs, upstream, lse, span_ids):
    T = queries.shape[1]
    rows = HEAD + 2 * T
    vmem = pl.BlockSpec(memory_space=pltpu.VMEM)
    return pl.pallas_call(
        functools.partial(kernel, mesh.shape["section"], mesh.shape["ctx"]),
        out_shape=(
            jax.ShapeDtypeStruct(queries.shape, BF16),
            jax.ShapeDtypeStruct(keys.shape, BF16),
            jax.ShapeDtypeStruct(values.shape, BF16),
        ),
        in_specs=[pl.BlockSpec(memory_space=pltpu.SMEM)] + [vmem] * 5 + [pl.BlockSpec(memory_space=pl.ANY)],
        out_specs=(vmem, vmem, vmem),
        scratch_shapes=[
            pltpu.VMEM((5, G, rows, D), BF16),
            pltpu.VMEM((G, T, R * D), BF16),
            pltpu.VMEM((G, D, R * T), F32),
            pltpu.VMEM((G, 8, R * T), F32),
            pltpu.VMEM((3, G, 2 * T, D), F32),
            pltpu.VMEM((4, G, 2 * T, D), BF16),
            pltpu.VMEM((4, G, 2 * T, D), BF16),
            pltpu.SemaphoreType.DMA((G,)),
            pltpu.SemaphoreType.DMA((G,)),
            pltpu.SemaphoreType.DMA((4, G)),
            pltpu.SemaphoreType.DMA((4, G)),
            pltpu.SemaphoreType.DMA((4, G)),
            pltpu.SemaphoreType.DMA((4, G)),
        ],
        compiler_params=pltpu.CompilerParams(
            collective_id=0, has_side_effects=True, vmem_limit_bytes=40 * 1024 * 1024
        ),
    )(span_ids, queries, keys, values, outputs, lse, upstream)


def solution(mesh):
    placed = (
        P("section", "ctx", None),
        P("section", "ctx", None),
        P("section", "ctx", None),
        P("section", "ctx", None),
        P("section", "ctx", None),
        P("section", None, "ctx"),
        P("ctx"),
    )
    return jax.shard_map(
        functools.partial(body, mesh),
        mesh=mesh,
        in_specs=placed,
        out_specs=(P("section", "ctx", None), P("section", "ctx", None), P("section", "ctx", None)),
        check_vma=False,
    )
```

time: 119 us -> 52.9 us (0.44)
  Pallas kernels: 0 us -> 43.5 us
  waiting for transfers between devices: 43.1 us -> 0 us
  starting transfers between devices: 20.8 us -> 0 us
  matrix products: 17.6 us -> 0 us
  other arithmetic: 11 us -> 0 us
  blocking collectives: 10.4 us -> 0 us
  local copies, waits for them, and re-layouts: 13.6 us -> 8.38 us
    pallas_call x0 -> x1, Pallas kernels: none -> 43.5 us  [body(): pl.pallas_call(functools.partial(kernel, mesh.shape['section'], mesh.shap...]
    ppermute x19 -> x0, waiting for transfers between devices: 43.1 us -> none  [from_behind(): return lax.ppermute(value, axis, pairs)]
    ppermute x19 -> x0, starting transfers between devices: 20.8 us -> none  [from_behind(): return lax.ppermute(value, axis, pairs)]
    dot_general x25 -> x0, matrix products: 17.6 us -> none  [the longest x5 6.65 us: block_terms(): jnp.einsum('qhgd,khd->hgqk', head_queries, key_now, preferred_element_typ...]
    unnamed x1 -> x0, blocking collectives: 10.4 us -> none
    add x11 -> x0, other arithmetic: 7.81 us -> none  [the longest x6 7.66 us: shard_positions(): return chosen * half + local % half]
    unnamed x1 -> x0, other arithmetic: 2.44 us -> none
    another operation x4 -> x0, local copies, waits for them, and re-layouts: 1.8 us -> none  [the longest x1 1.16 us: body(): outputs[0].reshape(query_rows, KEY_VALUE_HEADS, query_group, HEAD_WIDTH)]
  transfers between devices with their start and end apart: 19 -> 0, of which waited for: 11 -> 0; matrix products, arithmetic and copies ran while one was open for 32% -> 0% of each run, Pallas kernels for 0% -> 0%
where the time goes in v1:
time: 52.9 us; the launch traced here: 52.5 us
  Pallas kernels  43.5 us (82%)
  local copies, waits for them, and re-layouts  8.38 us (16%)
  between operations  0.66 us (1%)
    pallas_call x1, Pallas kernels, body(): pl.pallas_call(functools.partial(kernel, mesh.shape['section'], mesh.shap...  43.5 us
    unnamed x17, local copies, waits for them, and re-layouts  8.38 us

profile of v1, /device:TPU:0, one launch (start us, length us, event | category | flops | bytes accessed | tf_op | source)
XLA Modules:
  0.0 52.5 jit_solution(11076244013761232801)
XLA Ops:
  0.6 0.0 copy-start
  0.6 1.0 %copy-done = bf16[1,128,2048]{2,1,0:T(8,128)(2,1)S(1)} copy-done((bf16[1,128,2048]{2,1,0:T(8,128)(2,1)S(1)}, bf16[1,128,2048]{2,1,0:T(8,128)(2,1)}, u32[]{:S(2)}) %copy-start) | copy-done | bytes 524312
  1.7 0.0 copy-start.1
  1.7 1.0 %copy-done.1 = bf16[1,128,2048]{2,1,0:T(8,128)(2,1)S(1)} copy-done((bf16[1,128,2048]{2,1,0:T(8,128)(2,1)S(1)}, bf16[1,128,2048]{2,1,0:T(8,128)(2,1)}, u32[]{:S(2)}) %copy-start.1) | copy-done | bytes 524312
  2.7 0.0 copy-start.2
  2.7 1.0 %copy-done.2 = bf16[1,128,2048]{2,1,0:T(8,128)(2,1)S(1)} copy-done((bf16[1,128,2048]{2,1,0:T(8,128)(2,1)S(1)}, bf16[1,128,2048]{2,1,0:T(8,128)(2,1)}, u32[]{:S(2)}) %copy-start.2) | copy-done | bytes 524312
  3.8 0.0 copy-start.3
  3.8 0.9 %copy-done.3 = bf16[1,128,512]{2,1,0:T(8,128)(2,1)S(1)} copy-done((bf16[1,128,512]{2,1,0:T(8,128)(2,1)S(1)}, bf16[1,128,512]{2,1,0:T(8,128)(2,1)}, u32[]{:S(2)}) %copy-start.3) | copy-done | bytes 131096
  4.7 0.0 copy-start.4
  4.7 0.9 %copy-done.4 = bf16[1,128,512]{2,1,0:T(8,128)(2,1)S(1)} copy-done((bf16[1,128,512]{2,1,0:T(8,128)(2,1)S(1)}, bf16[1,128,512]{2,1,0:T(8,128)(2,1)}, u32[]{:S(2)}) %copy-start.4) | copy-done | bytes 131096
  5.6 0.0 copy-start.5
  5.6 0.7 %copy-done.5 = f32[1,16,128]{2,1,0:T(8,128)S(1)} copy-done((f32[1,16,128]{2,1,0:T(8,128)S(1)}, f32[1,16,128]{2,1,0:T(8,128)}, u32[]{:S(2)}) %copy-start.5) | copy-done | bytes 8216
  6.3 0.0 copy-start.6
  6.3 0.7 %copy-done.6 = s32[2]{0:T(128)S(1)} copy-done((s32[2]{0:T(128)S(1)}, s32[2]{0:T(128)}, u32[]{:S(2)}) %copy-start.6) | copy-done | bytes 32
  6.9 43.5 %shard_map.94 = (bf16[1,128,2048]{2,1,0:T(8,128)(2,1)S(1)}, bf16[1,128,512]{2,1,0:T(8,128)(2,1)S(1)}, bf16[1,128,512]{2,1,0:T(8,128)(2,1)S(1)}) custom-call(s32[2]{0:T(128)S(1)} %copy-done.6, bf16[1,128,2048]{2,1,0:T(8,128)(2,1)S(1)} %copy-done, bf16[1,128,512]{2,1,0:T(8,128)(2,1)S(1)} %copy-done.3, bf16[1,128,512]{2,1,0:T(8,128)(2,1)S(1)} %copy-done.4, ...), custom_call_target="tpu_custom_call" | custom-call | tf_op jit(solution)/shard_map/pallas_call | solution.py:235
  50.4 0.8 %copy.13 = bf16[1,128,2048]{2,1,0:T(8,128)(2,1)} copy(bf16[1,128,2048]{2,1,0:T(8,128)(2,1)S(1)} %get-tuple-element.6) | data formatting | bytes 1048576
  51.2 0.7 %copy.14 = bf16[1,128,512]{2,1,0:T(8,128)(2,1)} copy(bf16[1,128,512]{2,1,0:T(8,128)(2,1)S(1)} %get-tuple-element.7) | data formatting | bytes 262144
  51.9 0.7 %copy.15 = bf16[1,128,512]{2,1,0:T(8,128)(2,1)} copy(bf16[1,128,512]{2,1,0:T(8,128)(2,1)S(1)} %get-tuple-element.8) | data formatting | bytes 262144
Async XLA Ops:
  0.6 1.0 %copy-start = (bf16[1,128,2048]{2,1,0:T(8,128)(2,1)S(1)}, bf16[1,128,2048]{2,1,0:T(8,128)(2,1)}, u32[]{:S(2)}) copy-start(bf16[1,128,2048]{2,1,0:T(8,128)(2,1)} %q_ref.1) | copy-start | bytes 1572868
  1.7 1.0 %copy-start.1 = (bf16[1,128,2048]{2,1,0:T(8,128)(2,1)S(1)}, bf16[1,128,2048]{2,1,0:T(8,128)(2,1)}, u32[]{:S(2)}) copy-start(bf16[1,128,2048]{2,1,0:T(8,128)(2,1)} %o_ref.1) | copy-start | bytes 1572868
  2.7 1.0 %copy-start.2 = (bf16[1,128,2048]{2,1,0:T(8,128)(2,1)S(1)}, bf16[1,128,2048]{2,1,0:T(8,128)(2,1)}, u32[]{:S(2)}) copy-start(bf16[1,128,2048]{2,1,0:T(8,128)(2,1)} %up_ref.1) | copy-start | bytes 1572868
  3.8 0.9 %copy-start.3 = (bf16[1,128,512]{2,1,0:T(8,128)(2,1)S(1)}, bf16[1,128,512]{2,1,0:T(8,128)(2,1)}, u32[]{:S(2)}) copy-start(bf16[1,128,512]{2,1,0:T(8,128)(2,1)} %k_ref.1) | copy-start | bytes 393220
  4.7 0.9 %copy-start.4 = (bf16[1,128,512]{2,1,0:T(8,128)(2,1)S(1)}, bf16[1,128,512]{2,1,0:T(8,128)(2,1)}, u32[]{:S(2)}) copy-start(bf16[1,128,512]{2,1,0:T(8,128)(2,1)} %v_ref.1) | copy-start | bytes 393220
  5.6 0.7 %copy-start.5 = (f32[1,16,128]{2,1,0:T(8,128)S(1)}, f32[1,16,128]{2,1,0:T(8,128)}, u32[]{:S(2)}) copy-start(f32[1,16,128]{2,1,0:T(8,128)} %lse_ref.1) | copy-start | bytes 24580
  6.3 0.7 %copy-start.6 = (s32[2]{0:T(128)S(1)}, s32[2]{0:T(128)}, u32[]{:S(2)}) copy-start(s32[2]{0:T(128)} %span_ref.1) | copy-start | bytes 28

commit v2 on v1

--- a/solution.py
+++ b/solution.py
@@ -23,10 +23,11 @@
 
 
 def kernel(
-    sections, count, span_ref, q_ref, k_ref, v_ref, o_ref, lse_ref, up_ref,
+    sections, count, span_ref, q_hbm, k_hbm, v_hbm, o_hbm, lse_hbm, up_ref,
     dq_ref, dk_ref, dv_ref,
+    q_ref, o_ref, lse_ref,
     kv, do, dqt, delta, pacc, gsend, grecv,
-    up_s, up_r, kv_s, kv_r, g_s, g_r,
+    loc, kvloc, up_s, up_r, kv_s, kv_r, g_s, g_r,
 ):
     T = q_ref.shape[1]
     half = T // 2
@@ -39,22 +40,36 @@
     below = lax.rem(me + count - 2, count)
     partner = me + 1 - 2 * side
 
-    s0 = span_ref[0]
-    s1 = span_ref[1]
-
-    rows = lax.broadcasted_iota(jnp.int32, (HEAD, D), 0)
-    header = jnp.where(rows < HEAD // 2, s0, s1).astype(F32).astype(BF16)
-    for g in range(G):
-        kv[0, g, 0:HEAD, :] = header
-        kv[0, g, HEAD : HEAD + T, :] = k_ref[0, :, g * D : (g + 1) * D]
-        kv[0, g, HEAD + T : HEAD + 2 * T, :] = v_ref[0, :, g * D : (g + 1) * D]
-
     barrier = pltpu.get_barrier_semaphore()
     for axis, other in (
         ("ctx", above), ("ctx", below), ("ctx", partner),
         ("section", sec_prev), ("section", sec_next),
     ):
         pl.semaphore_signal(barrier, inc=1, device_id={axis: other}, device_id_type=MESH)
+
+    own = []
+    for g in range(G):
+        cols = slice(g * D, (g + 1) * D)
+        own.append((
+            pltpu.make_async_copy(k_hbm.at[0, :, cols], kv.at[0, g, HEAD : HEAD + T, :], kvloc.at[0, g]),
+            pltpu.make_async_copy(v_hbm.at[0, :, cols], kv.at[0, g, HEAD + T : HEAD + 2 * T, :], kvloc.at[1, g]),
+        ))
+        own[g][0].start()
+        own[g][1].start()
+    local = (
+        pltpu.make_async_copy(q_hbm, q_ref, loc.at[0]),
+        pltpu.make_async_copy(o_hbm, o_ref, loc.at[1]),
+        pltpu.make_async_copy(lse_hbm, lse_ref, loc.at[2]),
+    )
+    for copy in local:
+        copy.start()
+
+    s0 = span_ref[0]
+    s1 = span_ref[1]
+    rows = lax.broadcasted_iota(jnp.int32, (HEAD, D), 0)
+    header = jnp.where(rows < HEAD // 2, s0, s1).astype(F32).astype(BF16)
+    for g in range(G):
+        kv[0, g, 0:HEAD, :] = header
     pl.semaphore_wait(barrier, 5)
 
     def up_copy(g):
@@ -78,23 +93,21 @@
             device_id={"ctx": below if t in (C1, C2) else partner}, device_id_type=MESH,
         )
 
-    def loop(body):
-        def step(g, carry):
-            body(g)
-            return carry
-
-        lax.fori_loop(0, G, step, 0)
-
-    def start_all(g):
+    def send_own(g):
         kv_copy(C1, 0, g).start()
 
         @pl.when(side == 0)
         def _():
             kv_copy(X1, 0, g).start()
 
+    for g in range(G):
+        own[g][0].wait()
+        own[g][1].wait()
+        if g < 2:
+            send_own(g)
         up_copy(g).start()
-
-    loop(start_all)
+    for copy in local:
+        copy.wait()
 
     scale = D ** (-0.5)
     scale2 = scale * math.log2(math.e)
@@ -147,7 +160,7 @@
         gsend[t, g, T : 2 * T, :] = pair[1].astype(BF16)
         g_copy(t, g).start()
 
-    def phase1(g):
+    def relay(g):
         kv_copy(C1, 0, g).wait_recv()
         kv_copy(C2, 1, g).start()
 
@@ -158,6 +171,17 @@
         @pl.when(side == 1)
         def _():
             kv_copy(X1, 1, g).start()
+
+        @pl.when(g + 2 < G)
+        def _():
+            send_own(g + 2)
+
+    def work(g):
+        kv_copy(C2, 1, g).wait_recv()
+
+        @pl.when(side == 1)
+        def _():
+            kv_copy(X3, 2, g).start()
 
         up_copy(g).wait_recv()
         o4 = o_ref[0, :, pl.ds(pl.multiple_of(g * (R * D), R * D), R * D)].astype(F32)
@@ -166,34 +190,18 @@
             [jnp.sum(prod[:, j * D : (j + 1) * D].T, axis=0, keepdims=True) for j in range(R)], axis=1
         )
         keep(g, 0, block(g, 0, True))
-
-    loop(phase1)
-
-    def phase2(g):
-        kv_copy(C2, 1, g).wait_recv()
-
-        @pl.when(side == 1)
-        def _():
-            kv_copy(X3, 2, g).start()
-
         keep(g, 1, block(g, 1))
-
-    loop(phase2)
-
-    def phase3(g):
+        keep(g, 2, block(g, 2))
         kv_copy(X1, 0, g).wait_recv()
         pass_on(X1, g, block(g, 3))
         kv_copy(X3, 0, g).wait_recv()
         pass_on(X3, g, block(g, 4))
-        keep(g, 2, block(g, 2))
         total = dqt[g]
         dq_ref[0, :, pl.ds(pl.multiple_of(g * (R * D), R * D), R * D)] = jnp.concatenate(
             [total[:, j * T : (j + 1) * T].T for j in range(R)], axis=1
         ).astype(BF16)
 
-    loop(phase3)
-
-    def phase4(g):
+    def join(g):
         g_copy(X1, g).wait_recv()
         pacc[side, g] += grecv[X1, g].astype(F32)
         g_copy(X3, g).wait_recv()
@@ -201,31 +209,38 @@
         gsend[C2, g] = pacc[2, g].astype(BF16)
         g_copy(C2, g).start()
 
-    loop(phase4)
-
-    def phase5(g):
+    def descend(g):
         g_copy(C2, g).wait_recv()
         gsend[C1, g] = (pacc[1, g] + grecv[C2, g].astype(F32)).astype(BF16)
         g_copy(C1, g).start()
 
-    loop(phase5)
-
-    def phase6(g):
+    def home(g):
         g_copy(C1, g).wait_recv()
         total = (pacc[0, g] + grecv[C1, g].astype(F32)).astype(BF16)
         at = pl.ds(pl.multiple_of(g * D, D), D)
         dk_ref[0, :, at] = total[0:T]
         dv_ref[0, :, at] = total[T : 2 * T]
 
-    loop(phase6)
-
-    def finish(g):
+    def step(i, carry):
+        for lag, stage in enumerate((relay, work, join, descend, home)):
+            g = i - lag
+
+            @pl.when((g >= 0) & (g < G))
+            def _():
+                stage(g)
+
+        return carry
+
+    lax.fori_loop(0, G + 4, step, 0)
+
+    def finish(g, carry):
         up_copy(g).wait_send()
         for t in (C1, C2, X1, X3):
             kv_copy(t, 0, g).wait_send()
             g_copy(t, g).wait_send()
-
-    loop(finish)
+        return carry
+
+    lax.fori_loop(0, G, finish, 0)
 
 
 def body(mesh, queries, keys, values, outputs, upstream, lse, span_ids):
@@ -239,9 +254,12 @@
             jax.ShapeDtypeStruct(keys.shape, BF16),
             jax.ShapeDtypeStruct(values.shape, BF16),
         ),
-        in_specs=[pl.BlockSpec(memory_space=pltpu.SMEM)] + [vmem] * 5 + [pl.BlockSpec(memory_space=pl.ANY)],
+        in_specs=[pl.BlockSpec(memory_space=pltpu.SMEM)] + [pl.BlockSpec(memory_space=pltpu.HBM)] * 6,
         out_specs=(vmem, vmem, vmem),
         scratch_shapes=[
+            pltpu.VMEM(queries.shape, BF16),
+            pltpu.VMEM(outputs.shape, BF16),
+            pltpu.VMEM(lse.shape, F32),
             pltpu.VMEM((5, G, rows, D), BF16),
             pltpu.VMEM((G, T, R * D), BF16),
             pltpu.VMEM((G, D, R * T), F32),
@@ -249,6 +267,8 @@
             pltpu.VMEM((3, G, 2 * T, D), F32),
             pltpu.VMEM((4, G, 2 * T, D), BF16),
             pltpu.VMEM((4, G, 2 * T, D), BF16),
+            pltpu.SemaphoreType.DMA((3,)),
+            pltpu.SemaphoreType.DMA((2, G)),
             pltpu.SemaphoreType.DMA((G,)),
             pltpu.SemaphoreType.DMA((G,)),
             pltpu.SemaphoreType.DMA((4, G)),
@@ -257,7 +277,7 @@
             pltpu.SemaphoreType.DMA((4, G)),
         ],
         compiler_params=pltpu.CompilerParams(
-            collective_id=0, has_side_effects=True, vmem_limit_bytes=40 * 1024 * 1024
+            collective_id=0, has_side_effects=True, vmem_limit_bytes=60 * 1024 * 1024
         ),
     )(span_ids, queries, keys, values, outputs, lse, upstream)
 

time: 52.9 us -> 48.9 us (0.924)
  local copies, waits for them, and re-layouts: 8.38 us -> 3.53 us
  Pallas kernels: 43.5 us -> 44.5 us
    unnamed x17 -> x7, local copies, waits for them, and re-layouts: 8.38 us -> 3.53 us
    pallas_call x1, Pallas kernels: 43.5 us -> 44.5 us  [body(): pl.pallas_call(functools.partial(kernel, mesh.shape['section'], mesh.shap...]
where the time goes in v2:
time: 48.9 us; the launch traced here: 48.7 us
  Pallas kernels  44.5 us (91%)
  local copies, waits for them, and re-layouts  3.53 us (7%)
  between operations  0.65 us (1%)
    pallas_call x1, Pallas kernels, body(): pl.pallas_call(functools.partial(kernel, mesh.shape['section'], mesh.shap...  44.5 us
    unnamed x7, local copies, waits for them, and re-layouts  3.53 us

profile of v2, /device:TPU:0, one launch (start us, length us, event | category | flops | bytes accessed | tf_op | source)
XLA Modules:
  0.0 48.7 jit_solution(17535080394827740232)
XLA Ops:
  0.6 44.5 %shard_map.94 = (bf16[1,128,2048]{2,1,0:T(8,128)(2,1)}, bf16[1,128,512]{2,1,0:T(8,128)(2,1)}, bf16[1,128,512]{2,1,0:T(8,128)(2,1)}) custom-call(s32[2]{0:T(128)} %span_ref.1, bf16[1,128,2048]{2,1,0:T(8,128)(2,1)} %q_hbm.1, bf16[1,128,512]{2,1,0:T(8,128)(2,1)} %k_hbm.1, bf16[1,128,512]{2,1,0:T(8,128)(2,1)} %v_hbm.1, bf16[1,128,2048]{2,1,0:T(8,128)(2,1)} %o_hbm.1, ...), custom_call_target="tpu_custom_call" | custom-call | tf_op jit(solution)/shard_map/pallas_call | solution.py:250
  45.2 0.0 copy-start.1
  45.2 1.9 %copy.13 = bf16[1,128,2048]{2,1,0:T(8,128)(2,1)} copy(bf16[1,128,2048]{2,1,0:T(8,128)(2,1)} %get-tuple-element.6) | data formatting | bytes 1048576
  47.1 0.0 copy-done.1
  47.1 0.0 copy-start
  47.1 0.7 %copy.14 = bf16[1,128,512]{2,1,0:T(8,128)(2,1)} copy(bf16[1,128,512]{2,1,0:T(8,128)(2,1)S(1)} %copy-done.1) | data formatting | bytes 262144
  47.8 0.3 copy-done
  48.1 0.7 %copy.15 = bf16[1,128,512]{2,1,0:T(8,128)(2,1)} copy(bf16[1,128,512]{2,1,0:T(8,128)(2,1)S(1)} %copy-done) | data formatting | bytes 262144
Async XLA Ops:
  45.2 1.9 %copy-start.1 = (bf16[1,128,512]{2,1,0:T(8,128)(2,1)S(1)}, bf16[1,128,512]{2,1,0:T(8,128)(2,1)}, u32[]{:S(2)}) copy-start(bf16[1,128,512]{2,1,0:T(8,128)(2,1)} %get-tuple-element.7) | copy-start | bytes 393220
  47.1 1.0 %copy-start = (bf16[1,128,512]{2,1,0:T(8,128)(2,1)S(1)}, bf16[1,128,512]{2,1,0:T(8,128)(2,1)}, u32[]{:S(2)}) copy-start(bf16[1,128,512]{2,1,0:T(8,128)(2,1)} %get-tuple-element.8) | copy-start | bytes 393220

commit v3 on v2

--- a/solution.py
+++ b/solution.py
@@ -11,7 +11,11 @@
 G = 4
 R = 4
 D = 128
+AHEAD = 4
 HEAD = 16
+ORDER = (
+    ("a", 0), ("a", 1), ("a", 2), ("a", 3), ("b", 0), ("b", 1), ("b", 2), ("b", 3), ("w", 0), ("w", 1), ("j", 0), ("w", 2), ("j", 1), ("d", 0), ("w", 3), ("j", 2), ("d", 1), ("j", 3), ("d", 2), ("h", 0), ("d", 3), ("h", 1), ("h", 2), ("h", 3),
+)
 MESH = pl.DeviceIdType.MESH
 F32 = jnp.float32
 BF16 = jnp.bfloat16
@@ -103,7 +107,7 @@
     for g in range(G):
         own[g][0].wait()
         own[g][1].wait()
-        if g < 2:
+        if g < AHEAD:
             send_own(g)
         up_copy(g).start()
     for copy in local:
@@ -172,17 +176,17 @@
         def _():
             kv_copy(X1, 1, g).start()
 
-        @pl.when(g + 2 < G)
-        def _():
-            send_own(g + 2)
+        if g + AHEAD < G:
+            send_own(g + AHEAD)
+
+    def relay2(g):
+        kv_copy(C2, 1, g).wait_recv()
+
+        @pl.when(side == 1)
+        def _():
+            kv_copy(X3, 2, g).start()
 
     def work(g):
-        kv_copy(C2, 1, g).wait_recv()
-
-        @pl.when(side == 1)
-        def _():
-            kv_copy(X3, 2, g).start()
-
         up_copy(g).wait_recv()
         o4 = o_ref[0, :, pl.ds(pl.multiple_of(g * (R * D), R * D), R * D)].astype(F32)
         prod = o4 * do[g].astype(F32)
@@ -221,17 +225,9 @@
         dk_ref[0, :, at] = total[0:T]
         dv_ref[0, :, at] = total[T : 2 * T]
 
-    def step(i, carry):
-        for lag, stage in enumerate((relay, work, join, descend, home)):
-            g = i - lag
-
-            @pl.when((g >= 0) & (g < G))
-            def _():
-                stage(g)
-
-        return carry
-
-    lax.fori_loop(0, G + 4, step, 0)
+    stages = {"a": relay, "b": relay2, "w": work, "j": join, "d": descend, "h": home}
+    for name, g in ORDER:
+        stages[name](g)
 
     def finish(g, carry):
         up_copy(g).wait_send()

time: 48.9 us -> 47.7 us (0.975)
  Pallas kernels: 44.5 us -> 43.1 us
    pallas_call x1, Pallas kernels: 44.5 us -> 43.1 us  [body(): pl.pallas_call(functools.partial(kernel, mesh.shape['section'], mesh.shap...]
where the time goes in v3:
time: 47.7 us; the launch traced here: 47.3 us
  Pallas kernels  43.1 us (90%)
  local copies, waits for them, and re-layouts  3.53 us (7%)
  between operations  0.65 us (1%)
    pallas_call x1, Pallas kernels, body(): pl.pallas_call(functools.partial(kernel, mesh.shape['section'], mesh.shap...  43.1 us
    unnamed x7, local copies, waits for them, and re-layouts  3.53 us

profile of v3, /device:TPU:0, one launch (start us, length us, event | category | flops | bytes accessed | tf_op | source)
XLA Modules:
  0.0 47.3 jit_solution(16798496114722306971)
XLA Ops:
  0.6 43.1 %shard_map.94 = (bf16[1,128,2048]{2,1,0:T(8,128)(2,1)}, bf16[1,128,512]{2,1,0:T(8,128)(2,1)}, bf16[1,128,512]{2,1,0:T(8,128)(2,1)}) custom-call(s32[2]{0:T(128)} %span_ref.1, bf16[1,128,2048]{2,1,0:T(8,128)(2,1)} %q_hbm.1, bf16[1,128,512]{2,1,0:T(8,128)(2,1)} %k_hbm.1, bf16[1,128,512]{2,1,0:T(8,128)(2,1)} %v_hbm.1, bf16[1,128,2048]{2,1,0:T(8,128)(2,1)} %o_hbm.1, ...), custom_call_target="tpu_custom_call" | custom-call | tf_op jit(solution)/shard_map/pallas_call | solution.py:246
  43.8 0.0 copy-start.1
  43.8 1.9 %copy.13 = bf16[1,128,2048]{2,1,0:T(8,128)(2,1)} copy(bf16[1,128,2048]{2,1,0:T(8,128)(2,1)} %get-tuple-element.6) | data formatting | bytes 1048576
  45.7 0.0 copy-done.1
  45.7 0.0 copy-start
  45.7 0.7 %copy.14 = bf16[1,128,512]{2,1,0:T(8,128)(2,1)} copy(bf16[1,128,512]{2,1,0:T(8,128)(2,1)S(1)} %copy-done.1) | data formatting | bytes 262144
  46.4 0.3 copy-done
  46.7 0.7 %copy.15 = bf16[1,128,512]{2,1,0:T(8,128)(2,1)} copy(bf16[1,128,512]{2,1,0:T(8,128)(2,1)S(1)} %copy-done) | data formatting | bytes 262144
Async XLA Ops:
  43.8 1.9 %copy-start.1 = (bf16[1,128,512]{2,1,0:T(8,128)(2,1)S(1)}, bf16[1,128,512]{2,1,0:T(8,128)(2,1)}, u32[]{:S(2)}) copy-start(bf16[1,128,512]{2,1,0:T(8,128)(2,1)} %get-tuple-element.7) | copy-start | bytes 393220
  45.7 1.0 %copy-start = (bf16[1,128,512]{2,1,0:T(8,128)(2,1)S(1)}, bf16[1,128,512]{2,1,0:T(8,128)(2,1)}, u32[]{:S(2)}) copy-start(bf16[1,128,512]{2,1,0:T(8,128)(2,1)} %get-tuple-element.8) | copy-start | bytes 393220

commit v4 on v3

--- a/solution.py
+++ b/solution.py
@@ -14,7 +14,7 @@
 AHEAD = 4
 HEAD = 16
 ORDER = (
-    ("a", 0), ("a", 1), ("a", 2), ("a", 3), ("b", 0), ("b", 1), ("b", 2), ("b", 3), ("w", 0), ("w", 1), ("j", 0), ("w", 2), ("j", 1), ("d", 0), ("w", 3), ("j", 2), ("d", 1), ("j", 3), ("d", 2), ("h", 0), ("d", 3), ("h", 1), ("h", 2), ("h", 3),
+    ("a", 0), ("a", 1), ("a", 2), ("a", 3), ("b", 0), ("b", 1), ("b", 2), ("b", 3), ("w", 0), ("w", 1), ("w", 2), ("j", 0), ("w", 3), ("j", 1), ("d", 0), ("j", 2), ("d", 1), ("j", 3), ("d", 2), ("h", 0), ("d", 3), ("h", 1), ("h", 2), ("h", 3),
 )
 MESH = pl.DeviceIdType.MESH
 F32 = jnp.float32

time: 47.7 us -> 47.3 us (level)
  no operation moved by 1% of the time
where the time goes in v4:
time: 47.3 us; the launch traced here: 47.1 us
  Pallas kernels  42.9 us (91%)
  local copies, waits for them, and re-layouts  3.53 us (7%)
  between operations  0.65 us (1%)
    pallas_call x1, Pallas kernels, body(): pl.pallas_call(functools.partial(kernel, mesh.shape['section'], mesh.shap...  42.9 us
    unnamed x7, local copies, waits for them, and re-layouts  3.53 us

profile of v4, /device:TPU:0, one launch (start us, length us, event | category | flops | bytes accessed | tf_op | source)
XLA Modules:
  0.0 47.1 jit_solution(9149582534094953030)
XLA Ops:
  0.6 42.9 %shard_map.94 = (bf16[1,128,2048]{2,1,0:T(8,128)(2,1)}, bf16[1,128,512]{2,1,0:T(8,128)(2,1)}, bf16[1,128,512]{2,1,0:T(8,128)(2,1)}) custom-call(s32[2]{0:T(128)} %span_ref.1, bf16[1,128,2048]{2,1,0:T(8,128)(2,1)} %q_hbm.1, bf16[1,128,512]{2,1,0:T(8,128)(2,1)} %k_hbm.1, bf16[1,128,512]{2,1,0:T(8,128)(2,1)} %v_hbm.1, bf16[1,128,2048]{2,1,0:T(8,128)(2,1)} %o_hbm.1, ...), custom_call_target="tpu_custom_call" | custom-call | tf_op jit(solution)/shard_map/pallas_call | solution.py:246
  43.6 0.0 copy-start.1
  43.6 1.9 %copy.13 = bf16[1,128,2048]{2,1,0:T(8,128)(2,1)} copy(bf16[1,128,2048]{2,1,0:T(8,128)(2,1)} %get-tuple-element.6) | data formatting | bytes 1048576
  45.5 0.0 copy-done.1
  45.5 0.0 copy-start
  45.5 0.7 %copy.14 = bf16[1,128,512]{2,1,0:T(8,128)(2,1)} copy(bf16[1,128,512]{2,1,0:T(8,128)(2,1)S(1)} %copy-done.1) | data formatting | bytes 262144
  46.2 0.3 copy-done
  46.5 0.7 %copy.15 = bf16[1,128,512]{2,1,0:T(8,128)(2,1)} copy(bf16[1,128,512]{2,1,0:T(8,128)(2,1)S(1)} %copy-done) | data formatting | bytes 262144
Async XLA Ops:
  43.6 1.9 %copy-start.1 = (bf16[1,128,512]{2,1,0:T(8,128)(2,1)S(1)}, bf16[1,128,512]{2,1,0:T(8,128)(2,1)}, u32[]{:S(2)}) copy-start(bf16[1,128,512]{2,1,0:T(8,128)(2,1)} %get-tuple-element.7) | copy-start | bytes 393220
  45.5 1.0 %copy-start = (bf16[1,128,512]{2,1,0:T(8,128)(2,1)S(1)}, bf16[1,128,512]{2,1,0:T(8,128)(2,1)}, u32[]{:S(2)}) copy-start(bf16[1,128,512]{2,1,0:T(8,128)(2,1)} %get-tuple-element.8) | copy-start | bytes 393220
